TPU v7x, 32 devices: a whole 2x2x4 slice. The times are simulated.
32 devices in a mesh: rows: 8 (over z, x), cols: 4 (over y, core).
Axes of the slice: x: 2, y: 2, z: 4, core: 2. Of those that a mesh axis runs over, the one named last changes fastest.
Arguments:
- features: bfloat16 [768, 128, 512], P(None, 'rows', 'cols'), may hold values from -6 to 6
- labels: int32 [128, 512], P('rows', 'cols'), may hold values from 0 to 15
- w_input: bfloat16 [128, 768], replicated, may hold values from -0.21875 to 0.21875
- w_dilate4: bfloat16 [128, 1152], replicated, may hold values from -0.1875 to 0.1875
- w_dilate8: bfloat16 [128, 1152], replicated, may hold values from -0.1875 to 0.1875
- w_classes: bfloat16 [16, 128], replicated, may hold values from -0.5 to 0.5
Outputs:
- grad_input: float32 [128, 768], replicated
- grad_dilate4: float32 [128, 1152], replicated
- grad_dilate8: float32 [128, 1152], replicated
- grad_classes: float32 [16, 128], replicated
All inputs are finite; a program needn't handle non-finite values.
Results may differ from a plain program's by a relative error of at most 0.006.
Values may be sent and summed in bfloat16 or wider, within the bound.
A program may use at most 128 MiB of HBM per device.

v0:
```python
import jax
import jax.numpy as jnp
from jax import lax
from jax.sharding import PartitionSpec as P

loss_weight = 0.03125


def extended(shard, sides, width):
    for axis, dim in sides:
        count, length = (lax.axis_size(axis), shard.shape[dim])
        up = [(i, (i + 1) % count) for i in range(count - 1)]
        down = [(j, i) for i, j in up]
        last = lax.slice_in_dim(shard, length - width, length, axis=dim)
        first = lax.slice_in_dim(shard, 0, width, axis=dim)
        before = lax.ppermute(last, axis, up)
        after = lax.ppermute(first, axis, down)
        shard = jnp.concatenate([before, shard, after], axis=dim)
    return shard


def smooth(value):
    return value * jax.nn.sigmoid(value)


def slope(value):
    sig = jax.nn.sigmoid(value)
    return sig * (1.0 + value * (1.0 - sig))


def gather_taps(padded, dilation, anchor, sign, out_rows, out_cols):
    pieces = []
    for tap in range(9):
        top = anchor + sign * (tap // 3 - 1) * dilation
        left = anchor + sign * (tap % 3 - 1) * dilation
        pieces.append(padded[:, top : top + out_rows, left : left + out_cols])
    stacked = jnp.concatenate(pieces, 0)
    return stacked.reshape(stacked.shape[0], out_rows * out_cols)


def pixel_contract(left, right):
    return lax.dot_general(
        left, right, (((1,), (1,)), ((), ())), preferred_element_type=jnp.float32
    )


def flipped(weight):
    chans = weight.shape[0]
    return weight.reshape(chans, 9, chans).transpose(2, 1, 0).reshape(chans, 9 * chans)


def local(features, labels, w_input, w_dilate4, w_dilate8, w_classes):
    chans = features.shape[0]
    rows = features.shape[1]
    cols = features.shape[2]
    pixels = rows * cols
    middle = w_input.shape[0]
    classes = w_classes.shape[0]
    flat = features.reshape(chans, pixels)
    a1 = jnp.dot(w_input, flat, preferred_element_type=jnp.float32)
    h1 = smooth(a1).astype(jnp.bfloat16).reshape(middle, rows, cols)
    h1_wide = extended(h1, (("rows", 1), ("cols", 2)), 12)
    a2_wide = jnp.dot(
        w_dilate4,
        gather_taps(h1_wide, 4, 4, 1, rows + 16, cols + 16),
        preferred_element_type=jnp.float32,
    )
    row_pos = lax.axis_index("rows") * rows - 8 + jnp.arange(rows + 16, dtype=jnp.int32)
    col_pos = lax.axis_index("cols") * cols - 8 + jnp.arange(cols + 16, dtype=jnp.int32)
    row_ok = (row_pos >= 0) & (row_pos < rows * lax.axis_size("rows"))
    col_ok = (col_pos >= 0) & (col_pos < cols * lax.axis_size("cols"))
    inside = (row_ok[:, None] & col_ok[None, :]).astype(jnp.float32)
    a2_grid = a2_wide.reshape(middle, rows + 16, cols + 16)
    h2_pad = (smooth(a2_grid) * inside[None]).astype(jnp.bfloat16)
    h1_pad = h1_wide[:, 8:-8, 8:-8]
    h2_taps = gather_taps(h2_pad, 8, 8, 1, rows, cols)
    a3 = jnp.dot(w_dilate8, h2_taps, preferred_element_type=jnp.float32)
    h3 = smooth(a3).astype(jnp.bfloat16)
    logits = jnp.dot(w_classes, h3, preferred_element_type=jnp.float32)
    expo = jnp.exp(logits)
    prob = expo / jnp.sum(expo, axis=0, keepdims=True)
    onehot = (labels.reshape(1, pixels) == jnp.arange(classes, dtype=jnp.int32)[:, None]).astype(
        jnp.float32
    )
    g4 = (loss_weight * (prob - onehot)).astype(jnp.bfloat16)
    grad_classes = pixel_contract(g4, h3)
    back3 = lax.dot_general(
        w_classes, g4, (((0,), (0,)), ((), ())), preferred_element_type=jnp.float32
    )
    g3 = (back3 * slope(a3)).astype(jnp.bfloat16)
    grad_dilate8 = pixel_contract(g3, h2_taps)
    g3_grid = g3.reshape(middle, rows, cols)
    g3_wide = extended(g3_grid, (("rows", 1), ("cols", 2)), 12)
    back2_wide = jnp.dot(
        flipped(w_dilate8),
        gather_taps(g3_wide, 8, 8, -1, rows + 8, cols + 8),
        preferred_element_type=jnp.float32,
    )
    scale_grid = slope(a2_grid[:, 4:-4, 4:-4]) * inside[None, 4:-4, 4:-4]
    g2_pad = (back2_wide.reshape(middle, rows + 8, cols + 8) * scale_grid).astype(jnp.bfloat16)
    g2 = g2_pad[:, 4 : 4 + rows, 4 : 4 + cols].reshape(middle, pixels)
    grad_dilate4 = pixel_contract(g2, gather_taps(h1_pad, 4, 4, 1, rows, cols))
    back1 = jnp.dot(
        flipped(w_dilate4),
        gather_taps(g2_pad, 4, 4, -1, rows, cols),
        preferred_element_type=jnp.float32,
    )
    g1 = (back1 * slope(a1)).astype(jnp.bfloat16)
    grad_input = pixel_contract(g1, flat)
    grad_input, grad_dilate4, grad_dilate8, grad_classes = lax.psum(
        (grad_input, grad_dilate4, grad_dilate8, grad_classes), ("rows", "cols")
    )
    return (grad_input, grad_dilate4, grad_dilate8, grad_classes)


def solution(mesh):
    return jax.shard_map(
        local,
        mesh=mesh,
        in_specs=(P(None, "rows", "cols"), P("rows", "cols"), P(), P(), P(), P()),
        out_specs=(P(), P(), P(), P()),
        check_vma=False,
    )
```

profile of v0, /device:TPU:1, one launch (start us, length us, event | category | flops | bytes accessed | tf_op | source)
XLA Modules:
  0.0 333.7 jit_solution(14210163149096967699)
XLA Ops:
  8.1 2.6 fusion.2
  12.7 4.0 %collective-permute-start = (bf16[128,12,128]{2,0,1:T(8,128)(2,1)S(1)}, bf16[128,12,128]{2,0,1:T(8,128)(2,1)S(1)}, u32[]{:S(2)}, u32[]{:S(2)}) collective-permute-start(bf16[128,12,128]{2,0,1:T(8,128)(2,1)S(1)} %get-tuple-element.16), channel_id=1, source_target_pairs={{0,4},{4,8},{8,12},{12,16},{16,20},{20,24},{24,28},{1,5},{5,9},{9,... | collective-permute-start | bytes 1179656 | tf_op jit(solution)/shard_map/ppermute | solution.py:16
  19.1 13.7 %collective-permute-done = bf16[128,12,128]{2,0,1:T(8,128)(2,1)S(1)} collective-permute-done((bf16[128,12,128]{2,0,1:T(8,128)(2,1)S(1)}, bf16[128,12,128]{2,0,1:T(8,128)(2,1)S(1)}, u32[]{:S(2)}, u32[]{:S(2)}) %collective-permute-start) | collective-permute-done | bytes 393248 | tf_op jit(solution)/shard_map/ppermute | solution.py:16
  37.5 4.6 %collective-permute-start.2 = (bf16[128,40,12]{0,1,2:T(8,128)(2,1)S(1)}, bf16[128,40,12]{0,1,2:T(8,128)(2,1)S(1)}, u32[]{:S(2)}, u32[]{:S(2)}) collective-permute-start(bf16[128,40,12]{0,1,2:T(8,128)(2,1)S(1)} %copy.42), channel_id=1, source_target_pairs={{0,1},{1,2},{2,3},{4,5},{5,6},{6,7},{8,9},{9,10},{10,11},{12,13},{... | collective-permute-start | bytes 368648 | tf_op jit(solution)/shard_map/ppermute | solution.py:16
  44.8 2.4 collective-permute-start.3
  49.2 1.8 collective-permute-done.3
  51.6 2.8 pad_maximum_fusion
  56.0 2.4 slice_dynamic-update-slice_fusion.7
  58.4 2.5 slice_dynamic-update-slice_fusion.6
  62.4 2.4 slice_dynamic-update-slice_fusion.4
  64.9 2.4 slice_dynamic-update-slice_fusion.3
  68.9 2.4 slice_dynamic-update-slice_fusion.1
  71.3 2.4 slice_dynamic-update-slice_fusion
  73.7 20.0 %copy.46 = bf16[1152,32,144]{0,2,1:T(8,128)(2,1)} copy(bf16[1152,32,144]{2,0,1:T(8,128)(2,1)} %slice_dynamic-update-slice_fusion) | data formatting | bytes 21233664 | tf_op jit(solution)/shard_map/concatenate | solution.py:37
  93.7 5.7 %fusion.27 = f32[4608,128]{1,0:T(8,128)S(1)} fusion(bf16[1152,4608]{0,1:T(8,128)(2,1)} %bitcast.79, bf16[128,1152]{1,0:T(8,128)(2,1)S(1)} %copy-done.17), kind=kOutput, calls=%fused_computation.97 | convolution fusion | flops 1358954496 | bytes 13271040 | tf_op jit(solution)/shard_map/dot_general | solution.py:63
  108.3 4.9 %collective-permute-start.4 = (bf16[128,12,128]{0,2,1:T(8,128)(2,1)}, bf16[128,12,128]{0,2,1:T(8,128)(2,1)}, u32[]{:S(2)}, u32[]{:S(2)}) collective-permute-start(bf16[128,12,128]{0,2,1:T(8,128)(2,1)} %get-tuple-element.13), channel_id=1, source_target_pairs={{0,4},{4,8},{8,12},{12,16},{16,20},{20,24},{24,28},{1,5},{5,9},{9,... | collective-permute-start | bytes 1179656 | tf_op jit(solution)/shard_map/ppermute | solution.py:16
  114.5 2.0 fusion.13
  124.7 3.3 copy.69
  128.0 4.2 %fusion.29 = f32[128,1152]{1,0:T(8,128)} fusion(bf16[128,2048]{1,0:T(8,128)(2,1)} %fusion.8, bf16[1152,2048]{0,1:T(8,128)(2,1)} %bitcast.89), kind=kOutput, calls=%fused_computation.99 | convolution fusion | flops 603979776 | bytes 5832704 | tf_op jit(solution)/shard_map/dot_general | solution.py:42
  133.1 1.9 collective-permute-start.6
  135.0 3.6 %collective-permute-start.7 = (bf16[128,40,12]{0,2,1:T(8,128)(2,1)S(1)}, bf16[128,40,12]{0,2,1:T(8,128)(2,1)S(1)}, u32[]{:S(2)}, u32[]{:S(2)}) collective-permute-start(bf16[128,40,12]{0,2,1:T(8,128)(2,1)S(1)} %get-tuple-element.9), channel_id=1, source_target_pairs={{0,1},{1,2},{2,3},{4,5},{5,6},{6,7},{8,9},{9,10},{10,11},{12,13},{... | collective-permute-start | bytes 368648 | tf_op jit(solution)/shard_map/ppermute | solution.py:16
  140.9 3.0 maximum_maximum_fusion
  147.8 3.4 %fusion.28 = f32[3264,128]{1,0:T(8,128)} fusion(bf16[1152,3264]{0,1:T(8,128)(2,1)S(1)} %bitcast.82, bf16[128,1152]{0,1:T(8,128)(2,1)S(1)} %bitcast.93), kind=kOutput, calls=%fused_computation.98 | convolution fusion | flops 962592768 | bytes 9486336 | tf_op jit(solution)/shard_map/dot_general | solution.py:94
  151.2 3.4 %copy.55 = f32[128,24,136]{2,0,1:T(8,128)} copy(f32[128,24,136]{0,2,1:T(8,128)} %bitcast.87) | data formatting | bytes 3342336 | tf_op jit(solution)/shard_map/reshape | solution.py:100
  154.6 3.0 multiply_convert_fusion
  158.7 4.8 %convolution_bitcast_fusion = f32[128,1152]{1,0:T(8,128)} fusion(bf16[1152,16,128]{2,0,1:T(8,128)(2,1)} %fusion.10, bf16[128,24,136]{2,0,1:T(8,128)(2,1)S(1)} %multiply_convert_fusion), kind=kOutput, calls=%fused_computation.8 | convolution fusion | flops 603979776 | bytes 5832704 | tf_op jit(solution)/shard_map/dot_general | solution.py:42
  171.6 7.1 %copy.56 = bf16[1152,16,128]{0,2,1:T(8,128)(2,1)} copy(bf16[1152,16,128]{2,0,1:T(8,128)(2,1)} %slice_dynamic-update-slice_fusion.18) | data formatting | bytes 9437184 | tf_op jit(solution)/shard_map/concatenate | solution.py:37
  178.8 7.0 %fusion = f32[128,768]{1,0:T(8,128)} fusion(bf16[96,8,16,128]{3,2,1,0:T(8,128)(2,1)} %bitcast.92, bf16[1152,2048]{0,1:T(8,128)(2,1)} %bitcast.90, bf16[128,1152]{0,1:T(8,128)(2,1)S(1)} %bitcast.96, f32[128,2048]{1,0:T(8,128)S(1)} %copy-done.8), kind=kOutput, calls=%fused_computation | convolution fusion | flops 1008992256 | bytes 9601024 | tf_op jit(solution)/shard_map/dot_general | solution.py:42
  186.1 41.8 %psum.31 = f32[16,128]{1,0:T(8,128)} all-reduce(f32[16,128]{1,0:T(8,128)S(1)} %fusion.20), channel_id=1, replica_groups=mesh['rows'=8,'cols'=4] {'rows','cols'}, use_global_device_ids=true, to_apply=%region_4.0 | all-reduce | flops 2048 | bytes 16384 | tf_op jit(solution)/shard_map/psum | solution.py:110
  227.9 93.0 %all-reduce.3.cloned.1.call-done = (f32[128,768]{1,0:T(8,128)}, f32[128,1152]{1,0:T(8,128)}, f32[128,1152]{1,0:T(8,128)}) async-done(((f32[128,768]{1,0:T(8,128)}, f32[128,1152]{1,0:T(8,128)}, f32[128,1152]{1,0:T(8,128)}), (f32[128,768]{1,0:T(8,128)}, f32[128,1152]{1,0:T(8,128)}, f32[128,1152]{1,0:T(8,128)})) %all-reduce.3.cloned.1.call-update) | async-done | bytes 1572880 | tf_op jit(solution)/shard_map/psum | solution.py:110
  322.7 1.9 copy.131
  324.6 1.9 copy.132
  (127 shorter events, 56.5 us)
Async XLA Ops:
  7.2 0.9 copy-start
  7.2 313.8 %all-reduce.3.cloned.1.call-start = ((), (), s32[]{:S(2)}) async-start(), calls=%async_computation | async-start | bytes 3145728 | tf_op jit(solution)/shard_map/psum | solution.py:110
  8.1 9.9 %copy-start.20 = (bf16[128,1152]{1,0:T(8,128)(2,1)S(1)}, bf16[128,1152]{1,0:T(8,128)(2,1)}, u32[]{:S(2)}) copy-start(bf16[128,1152]{1,0:T(8,128)(2,1)} %param.10) | copy-start | bytes 884740
  10.7 22.5 %copy-start.6 = (f32[128,2048]{1,0:T(8,128)}, f32[128,2048]{1,0:T(8,128)S(1)}, u32[]{:S(2)}) copy-start(f32[128,2048]{1,0:T(8,128)S(1)} %fusion.2) | copy-start | bytes 3145732
  11.0 0.8 copy-start.10
  12.7 20.1 %collective-permute-start = (bf16[128,12,128]{2,0,1:T(8,128)(2,1)S(1)}, bf16[128,12,128]{2,0,1:T(8,128)(2,1)S(1)}, u32[]{:S(2)}, u32[]{:S(2)}) collective-permute-start(bf16[128,12,128]{2,0,1:T(8,128)(2,1)S(1)} %get-tuple-element.16), channel_id=1, source_target_pairs={{0,4},{4,8},{8,12},{12,16},{16,20},{20,24},{24,28},{1,5},{5,9},{9,... | collective-permute-start | bytes 1179656 | tf_op jit(solution)/shard_map/ppermute | solution.py:16
  16.7 16.5 %collective-permute-start.1 = (bf16[128,12,128]{2,0,1:T(8,128)(2,1)}, bf16[128,12,128]{2,0,1:T(8,128)(2,1)S(1)}, u32[]{:S(2)}, u32[]{:S(2)}) collective-permute-start(bf16[128,12,128]{2,0,1:T(8,128)(2,1)} %get-tuple-element.15), channel_id=1, source_target_pairs={{4,0},{8,4},{12,8},{16,12},{20,16},{24,20},{28,24},{5,1},{9,5},{13... | collective-permute-start | bytes 1179656 | tf_op jit(solution)/shard_map/ppermute | solution.py:17
  32.8 2.9 copy-start.15
  37.5 9.8 %collective-permute-start.2 = (bf16[128,40,12]{0,1,2:T(8,128)(2,1)S(1)}, bf16[128,40,12]{0,1,2:T(8,128)(2,1)S(1)}, u32[]{:S(2)}, u32[]{:S(2)}) collective-permute-start(bf16[128,40,12]{0,1,2:T(8,128)(2,1)S(1)} %copy.42), channel_id=1, source_target_pairs={{0,1},{1,2},{2,3},{4,5},{5,6},{6,7},{8,9},{9,10},{10,11},{12,13},{... | collective-permute-start | bytes 368648 | tf_op jit(solution)/shard_map/ppermute | solution.py:16
  44.8 6.2 %collective-permute-start.3 = (bf16[128,40,12]{0,1,2:T(8,128)(2,1)S(1)}, bf16[128,40,12]{0,1,2:T(8,128)(2,1)S(1)}, u32[]{:S(2)}, u32[]{:S(2)}) collective-permute-start(bf16[128,40,12]{0,1,2:T(8,128)(2,1)S(1)} %copy.43), channel_id=1, source_target_pairs={{1,0},{2,1},{3,2},{5,4},{6,5},{7,6},{9,8},{10,9},{11,10},{13,12},{... | collective-permute-start | bytes 368648 | tf_op jit(solution)/shard_map/ppermute | solution.py:17
  47.9 1.3 copy-start.2
  73.7 20.0 %copy-start.17 = (bf16[128,1152]{1,0:T(8,128)(2,1)S(1)}, bf16[128,1152]{1,0:T(8,128)(2,1)}, u32[]{:S(2)}) copy-start(bf16[128,1152]{1,0:T(8,128)(2,1)} %param.9) | copy-start | bytes 884740
  99.4 1.4 copy-start.4
  100.8 1.0 copy-start.21
  101.7 2.1 copy-start.12
  101.8 2.1 copy-start.23
  101.8 2.9 copy-start.24
  107.3 10.4 %copy-start.3 = (bf16[128,40,12]{2,0,1:T(8,128)(2,1)S(1)}, bf16[128,40,12]{2,0,1:T(8,128)(2,1)}, u32[]{:S(2)}) copy-start(bf16[128,40,12]{2,0,1:T(8,128)(2,1)} %copy-done.2) | copy-start | bytes 368644
  108.3 23.8 %collective-permute-start.4 = (bf16[128,12,128]{0,2,1:T(8,128)(2,1)}, bf16[128,12,128]{0,2,1:T(8,128)(2,1)}, u32[]{:S(2)}, u32[]{:S(2)}) collective-permute-start(bf16[128,12,128]{0,2,1:T(8,128)(2,1)} %get-tuple-element.13), channel_id=1, source_target_pairs={{0,4},{4,8},{8,12},{12,16},{16,20},{20,24},{24,28},{1,5},{5,9},{9,... | collective-permute-start | bytes 1179656 | tf_op jit(solution)/shard_map/ppermute | solution.py:16
  113.2 18.9 %collective-permute-start.5 = (bf16[128,12,128]{0,2,1:T(8,128)(2,1)}, bf16[128,12,128]{0,2,1:T(8,128)(2,1)}, u32[]{:S(2)}, u32[]{:S(2)}) collective-permute-start(bf16[128,12,128]{0,2,1:T(8,128)(2,1)} %get-tuple-element.14), channel_id=1, source_target_pairs={{4,0},{8,4},{12,8},{16,12},{20,16},{24,20},{28,24},{5,1},{9,5},{13... | collective-permute-start | bytes 1179656 | tf_op jit(solution)/shard_map/ppermute | solution.py:17
  116.5 2.4 copy-start.7
  120.0 2.4 copy-start.11
  120.0 2.4 copy-start.14
  120.0 3.4 %copy-start.5 = (f32[4608,128]{1,0:T(8,128)S(1)}, f32[4608,128]{1,0:T(8,128)}, u32[]{:S(2)}) copy-start(f32[4608,128]{1,0:T(8,128)} %copy-done.4) | copy-start | bytes 7077892
  133.1 6.8 %collective-permute-start.6 = (bf16[128,40,12]{0,2,1:T(8,128)(2,1)S(1)}, bf16[128,40,12]{0,2,1:T(8,128)(2,1)S(1)}, u32[]{:S(2)}, u32[]{:S(2)}) collective-permute-start(bf16[128,40,12]{0,2,1:T(8,128)(2,1)S(1)} %get-tuple-element.10), channel_id=1, source_target_pairs={{1,0},{2,1},{3,2},{5,4},{6,5},{7,6},{9,8},{10,9},{11,10},{13,12},{... | collective-permute-start | bytes 368648 | tf_op jit(solution)/shard_map/ppermute | solution.py:17
  135.0 5.9 %collective-permute-start.7 = (bf16[128,40,12]{0,2,1:T(8,128)(2,1)S(1)}, bf16[128,40,12]{0,2,1:T(8,128)(2,1)S(1)}, u32[]{:S(2)}, u32[]{:S(2)}) collective-permute-start(bf16[128,40,12]{0,2,1:T(8,128)(2,1)S(1)} %get-tuple-element.9), channel_id=1, source_target_pairs={{0,1},{1,2},{2,3},{4,5},{5,6},{6,7},{8,9},{9,10},{10,11},{12,13},{... | collective-permute-start | bytes 368648 | tf_op jit(solution)/shard_map/ppermute | solution.py:16
  146.8 1.0 copy-start.16
  151.2 3.4 %copy-start.9 = (f32[128,24,136]{2,0,1:T(8,128)S(1)}, f32[128,24,136]{2,0,1:T(8,128)}, u32[]{:S(2)}) copy-start(f32[128,24,136]{2,0,1:T(8,128)} %copy.69) | copy-start | bytes 5013508
  171.6 7.1 %copy-start.8 = (f32[128,2048]{1,0:T(8,128)S(1)}, f32[128,2048]{1,0:T(8,128)}, u32[]{:S(2)}) copy-start(f32[128,2048]{1,0:T(8,128)} %copy-done.6) | copy-start | bytes 3145732
  171.6 7.1 %copy-start.22 = (bf16[128,9,128]{0,2,1:T(8,128)(2,1)S(1)}, bf16[128,9,128]{0,2,1:T(8,128)(2,1)}, u32[]{:S(2)}) copy-start(bf16[128,9,128]{0,2,1:T(8,128)(2,1)} %copy.58) | copy-start | bytes 884740
  178.7 7.1 %copy-start.19 = (bf16[128,2048]{1,0:T(8,128)(2,1)S(1)}, bf16[128,2048]{1,0:T(8,128)(2,1)}, u32[]{:S(2)}) copy-start(bf16[128,2048]{1,0:T(8,128)(2,1)} %copy-done.18) | copy-start | bytes 1572868
  178.7 147.8 %copy-start.1 = (bf16[128,768]{1,0:T(8,128)(2,1)S(1)}, bf16[128,768]{1,0:T(8,128)(2,1)}, u32[]{:S(2)}) copy-start(bf16[128,768]{1,0:T(8,128)(2,1)} %param.8) | copy-start | bytes 589828
  (2 other events, 1.6 us)
Sparse Core Ops, SparseCore 0:
  185.9 134.9 all-reduce.2
where the time goes:
time: 340 us; the launch traced here: 334 us
  waiting for transfers between devices  110 us (32%)
  local copies, waits for them, and re-layouts  88.1 us (26%)
  blocking collectives  41.8 us (12%)
  matrix products  31.1 us (9%)
  other arithmetic  24.2 us (7%)
  starting transfers between devices  24 us (7%)
  between operations  14.8 us (4%)
    psum x1, waiting for transfers between devices, local(): lax.psum((grad_input, grad_dilate4, grad_dilate8, grad_classes), ('rows',...  93 us
    unnamed x89, local copies, waits for them, and re-layouts  42.3 us
    psum x1, blocking collectives, local(): lax.psum((grad_input, grad_dilate4, grad_dilate8, grad_classes), ('rows',...  41.8 us
    concatenate x6, local copies, waits for them, and re-layouts, gather_taps(): stacked = jnp.concatenate(pieces, 0)  30.8 us
    ppermute x4, starting transfers between devices, extended(): before = lax.ppermute(last, axis, up)  17 us
    dot_general x4, matrix products, pixel_contract(): lax.dot_general(left, right, (((1,), (1,)), ((), ())), preferred_element_...  16.2 us
    ppermute x4, waiting for transfers between devices, extended(): before = lax.ppermute(last, axis, up)  14.7 us
    unnamed x9, other arithmetic  10.4 us
  transfers between devices with their start and end apart: 9, of which 4 were waited for; matrix products, arithmetic and copies ran while one was open for 8% of the time, Pallas kernels for 0%

commit v1 on v0

v1 whole, which is shorter than its diff:
```python
import functools

import jax
import jax.numpy as jnp
from jax import lax
from jax.experimental import pallas as pl
from jax.experimental.pallas import tpu as pltpu
from jax.sharding import PartitionSpec as P

loss_weight = 0.03125
MESH = pl.DeviceIdType.MESH
BF = jnp.bfloat16
F32 = jnp.float32
HALO = 12
SIDE = 16


def nn(a, b):
    return lax.dot_general(a, b, (((1,), (0,)), ((), ())), preferred_element_type=F32)


def nt(a, b):
    return lax.dot_general(a, b, (((1,), (1,)), ((), ())), preferred_element_type=F32)


def tn(a, b):
    return lax.dot_general(a, b, (((0,), (0,)), ((), ())), preferred_element_type=F32)


def act(a):
    sig = 1.0 / (1.0 + jnp.exp(-a))
    return a * sig, sig * (1.0 + a * (1.0 - sig))


def flat2(v):
    return v.reshape(v.shape[0] * v.shape[1], v.shape[2])


class Halo:
    def __init__(self, buf, send, recv, me, counts, rows, cols):
        self.items = []
        (r, c), (nr, nc) = me, counts
        index = 0
        for dr in (-1, 1, 0):
            for dc in (0, -1, 1):
                if dr == 0 and dc == 0:
                    continue
                sr, dst_r, n_r = {
                    -1: (HALO, HALO + rows, HALO),
                    0: (HALO, HALO, rows),
                    1: (rows, 0, HALO),
                }[dr]
                sc, dst_c, n_c = {
                    -1: (SIDE, SIDE + cols, SIDE),
                    0: (SIDE, SIDE, cols),
                    1: (cols, 0, SIDE),
                }[dc]
                to_ok = self.inside(r + dr, nr) & self.inside(c + dc, nc)
                from_ok = self.inside(r - dr, nr) & self.inside(c - dc, nc)
                copy = functools.partial(
                    pltpu.make_async_remote_copy,
                    src_ref=buf.at[pl.ds(sr, n_r), pl.ds(sc, n_c), :],
                    dst_ref=buf.at[pl.ds(dst_r, n_r), pl.ds(dst_c, n_c), :],
                    send_sem=send.at[index],
                    recv_sem=recv.at[index],
                    device_id=(r + dr, c + dc),
                    device_id_type=MESH,
                )
                self.items.append((copy, to_ok, from_ok))
                index += 1

    @staticmethod
    def inside(i, n):
        return (i >= 0) & (i < n)

    def start(self):
        for copy, to_ok, _ in self.items:
            pl.when(to_ok)(lambda copy=copy: copy().start())

    def wait_recv(self):
        for copy, _, from_ok in self.items:
            pl.when(from_ok)(lambda copy=copy: copy().wait_recv())

    def wait_send(self):
        for copy, to_ok, _ in self.items:
            pl.when(to_ok)(lambda copy=copy: copy().wait_send())


class Reduce:
    def __init__(self, bufs, me, counts):
        self.snd, self.rc1, self.s2, self.rc2, self.ag, self.send, self.recv = bufs
        self.me, self.counts = me, counts
        total = self.snd.shape[0]
        self.blk = total // counts[1]
        self.piece = self.blk // counts[0]
        self.sem = 0
        self.copies = []

    def push(self, src, dst, device):
        copy = pltpu.make_async_remote_copy(
            src_ref=src,
            dst_ref=dst,
            send_sem=self.send.at[self.sem],
            recv_sem=self.recv.at[self.sem],
            device_id=device,
            device_id_type=MESH,
        )
        self.sem += 1
        copy.start()
        self.copies.append(copy)
        return copy

    def at(self, index, size):
        return pl.ds(pl.multiple_of(index * size, 16), size)

    def phase1(self):
        (r, c), (_, nc) = self.me, self.counts
        self.now = [
            self.push(
                self.snd.at[self.at(lax.rem(c + k, nc), self.blk), :],
                self.rc1.at[k - 1],
                (r, lax.rem(c + k, nc)),
            )
            for k in range(1, nc)
        ]

    def phase2(self):
        (r, c), (nr, nc) = self.me, self.counts
        acc = self.snd[self.at(c, self.blk), :].astype(F32)
        for k, copy in enumerate(self.now):
            copy.wait_recv()
            acc = acc + self.rc1[k].astype(F32)
        self.s2[...] = acc.astype(BF)
        self.now = [
            self.push(
                self.s2.at[self.at(lax.rem(r + k, nr), self.piece), :],
                self.rc2.at[k - 1],
                (lax.rem(r + k, nr), c),
            )
            for k in range(1, nr)
        ]

    def phase3(self):
        (r, c), (nr, nc) = self.me, self.counts
        acc = self.s2[self.at(r, self.piece), :].astype(F32)
        for k, copy in enumerate(self.now):
            copy.wait_recv()
            acc = acc + self.rc2[k].astype(F32)
        spot = self.at(c * nr + r, self.piece)
        self.ag[spot, :] = acc.astype(BF)
        self.now = [
            self.push(self.ag.at[spot, :], self.ag.at[spot, :], (lax.rem(r + k, nr), c))
            for k in range(1, nr)
        ]

    def phase4(self):
        (r, c), (_, nc) = self.me, self.counts
        for copy in self.now:
            copy.wait_recv()
        spot = self.at(c, self.blk)
        self.now = [
            self.push(self.ag.at[spot, :], self.ag.at[spot, :], (r, lax.rem(c + k, nc)))
            for k in range(1, nc)
        ]

    def finish(self):
        for copy in self.now:
            copy.wait_recv()

    def drain(self):
        for copy in self.copies:
            copy.wait_send()


def kernel(counts, rows, cols, *refs):
    (flat_ref, lab_ref, wi_ref, w4_ref, w8_ref, wc_ref, oi_ref, o4_ref, o8_ref, oc_ref) = refs[:10]
    (w1, x4, s1, s2, h2, x8, s3, w3, xg, g2p, g2o, xg4, g1, wt4, wt8) = refs[10:25]
    hs1, hr1, hs2, hr2 = refs[25:29]
    bufs_a, bufs_b = refs[29:36], refs[36:43]
    nr, nc = counts
    me = (lax.axis_index("rows"), lax.axis_index("cols"))
    r, c = me
    mid = wi_ref.shape[0]
    chans = wi_ref.shape[1]
    classes = wc_ref.shape[0]
    wide = cols + 16

    w1[...] = jnp.zeros_like(w1)
    w3[...] = jnp.zeros_like(w3)
    barrier = pltpu.get_barrier_semaphore()
    partners = [(lax.rem(r + k, nr), c) for k in range(1, nr)]
    partners += [(r, lax.rem(c + k, nc)) for k in range(1, nc)]
    partners += [(lax.rem(r + dr, nr), lax.rem(c + dc, nc)) for dr in (1, nr - 1) for dc in (1, nc - 1)]
    for device in partners:
        pl.semaphore_signal(barrier, inc=1, device_id=device, device_id_type=MESH)

    for t in range(9):
        wt4[(8 - t) * mid : (9 - t) * mid, :] = w4_ref[:, t * mid : (t + 1) * mid]
        wt8[(8 - t) * mid : (9 - t) * mid, :] = w8_ref[:, t * mid : (t + 1) * mid]

    def first(y, _):
        part = flat_ref[:, pl.ds(pl.multiple_of(y * 4 * cols, 128), 4 * cols)]
        a1 = nn(wi_ref[...], part).T
        h, s = act(a1)
        w1[pl.ds(HALO + 4 * y, 4), SIDE : SIDE + cols, :] = h.astype(BF).reshape(4, cols, mid)
        s1[pl.ds(4 * y, 4)] = s.reshape(4, cols, mid)
        return 0

    lax.fori_loop(0, rows // 4, first, 0)

    pl.semaphore_wait(barrier, len(partners))

    halo1 = Halo(w1, hs1, hr1, me, counts, rows, cols)
    halo1.start()
    halo1.wait_recv()

    def shift_into(dst, src, starts, width):
        for k, start in enumerate(starts):
            piece = src[:, start : start + width, :]
            dst[:, :, k * mid : (k + 1) * mid] = piece

    shift_into(x4, w1, (4, 8, 12), wide)

    def taps(x, base, step, count):
        return flat2(
            jnp.concatenate([x[pl.ds(base + step * k, count)] for k in range(3)], axis=-1)
        )

    def mask(row0, count):
        rp = r * rows + row0 + lax.broadcasted_iota(jnp.int32, (count, wide, mid), 0)
        cp = c * cols - 8 + lax.broadcasted_iota(jnp.int32, (count, wide, mid), 1)
        ok = (rp >= 0) & (rp < rows * nr) & (cp >= 0) & (cp < cols * nc)
        return ok.astype(F32)

    def second(b, _):
        a2 = nt(taps(x4, 8 * b, 4, 8), w4_ref[...])
        h, s = act(a2)
        m = mask(8 * b - 8, 8)
        h2[pl.ds(8 * b, 8)] = (h.reshape(8, wide, mid) * m).astype(BF)
        s2[pl.ds(8 * b, 8)] = s.reshape(8, wide, mid) * m
        return 0

    lax.fori_loop(0, (rows + 16) // 8, second, 0)
    shift_into(x8, h2, (0, 8, 16), cols)

    red_a = Reduce(bufs_a, me, counts)
    red_b = Reduce(bufs_b, me, counts)

    gc = jnp.zeros((classes, mid), F32)
    for b in range(rows // 8):
        a3 = nt(taps(x8, 8 * b, 8, 8), w8_ref[...])
        h3, s3v = act(a3)
        h3 = h3.astype(BF)
        expo = jnp.exp(nt(wc_ref[...], h3))
        prob = expo / jnp.sum(expo, axis=0, keepdims=True)
        label = jnp.concatenate(
            [
                jnp.broadcast_to(lab_ref[8 * b + j : 8 * b + j + 1, :], (classes, cols))
                for j in range(8)
            ],
            axis=1,
        )
        onehot = (label == lax.broadcasted_iota(jnp.int32, label.shape, 0)).astype(F32)
        g4 = (loss_weight * (prob - onehot)).astype(BF)
        gc = gc + nn(g4, h3)
        g3 = (tn(g4, wc_ref[...]) * s3v).astype(BF)
        w3[HALO + 8 * b : HALO + 8 * b + 8, SIDE : SIDE + cols, :] = g3.reshape(8, cols, mid)

    halo2 = Halo(w3, hs2, hr2, me, counts, rows, cols)
    halo2.start()

    def zero_tail(red, used):
        total = red.snd.shape[0]
        if total > used:
            red.snd[used:, :] = jnp.zeros((total - used, mid), BF)

    g3_t = flat2(w3[HALO : HALO + rows, SIDE : SIDE + cols, :]).T
    for ky in range(3):
        block = nn(g3_t, flat2(x8[8 * ky : 8 * ky + rows]))
        for kx in range(3):
            t = 3 * ky + kx
            red_a.snd[t * mid : (t + 1) * mid, :] = block[:, kx * mid : (kx + 1) * mid].astype(BF)
    red_a.snd[9 * mid : 9 * mid + classes, :] = gc.astype(BF)
    zero_tail(red_a, 9 * mid + classes)
    red_a.phase1()

    halo2.wait_recv()
    shift_into(xg, w3, (0, 8, 16), wide)

    def third(b, _):
        back = nn(taps(xg, 8 * b, 8, 8), wt8[...])
        g2p[pl.ds(8 * b, 8)] = (back.reshape(8, wide, mid) * s2[pl.ds(8 * b + 4, 8)]).astype(BF)
        return 0

    lax.fori_loop(0, (rows + 8) // 8, third, 0)
    red_a.phase2()

    shift_into(xg4, g2p, (4, 8, 12), cols)
    spot = lax.broadcasted_iota(jnp.int32, (rows, wide, mid), 1)
    own = (spot >= 8) & (spot < 8 + cols)
    g2o[...] = jnp.where(own, g2p[4 : 4 + rows].astype(F32), 0.0).astype(BF)

    g2_t = flat2(g2o[...]).T
    for ky in range(3):
        block = nn(g2_t, flat2(x4[8 + 4 * ky : 8 + 4 * ky + rows]))
        for kx in range(3):
            t = 3 * ky + kx
            red_b.snd[t * mid : (t + 1) * mid, :] = block[:, kx * mid : (kx + 1) * mid].astype(BF)
    red_a.phase3()

    def fourth(b, _):
        back = nn(taps(xg4, 8 * b, 4, 8), wt4[...])
        s = flat2(s1[pl.ds(8 * b, 8)])
        g1[pl.ds(pl.multiple_of(b * 8 * cols, 128), 8 * cols), :] = (back * s).astype(BF)
        return 0

    lax.fori_loop(0, rows // 8, fourth, 0)
    base = 9 * mid
    gi = nn(flat_ref[...], g1[...])
    for k in range(chans // mid):
        block = gi[k * mid : (k + 1) * mid, :].T
        red_b.snd[base + k * mid : base + (k + 1) * mid, :] = block.astype(BF)
    zero_tail(red_b, base + chans)
    red_b.phase1()
    red_a.phase4()
    red_b.phase2()
    red_a.finish()
    for t in range(9):
        o8_ref[:, t * mid : (t + 1) * mid] = red_a.ag[t * mid : (t + 1) * mid, :].astype(F32)
    oc_ref[...] = red_a.ag[9 * mid : 9 * mid + classes, :].astype(F32)
    red_b.phase3()
    red_b.phase4()
    red_b.finish()
    for t in range(9):
        o4_ref[:, t * mid : (t + 1) * mid] = red_b.ag[t * mid : (t + 1) * mid, :].astype(F32)
    for k in range(chans // mid):
        lo = base + k * mid
        oi_ref[:, k * mid : (k + 1) * mid] = red_b.ag[lo : lo + mid, :].astype(F32)
    halo1.wait_send()
    halo2.wait_send()
    red_a.drain()
    red_b.drain()


def reduce_scratch(used, counts):
    nr, nc = counts
    unit = 16 * nr * nc
    total = -(-used // unit) * unit
    blk = total // nc
    piece = blk // nr
    sems = 2 * (nr - 1) + 2 * (nc - 1)
    return [
        pltpu.VMEM((total, 128), BF),
        pltpu.VMEM((max(nc - 1, 1), blk, 128), BF),
        pltpu.VMEM((blk, 128), BF),
        pltpu.VMEM((max(nr - 1, 1), piece, 128), BF),
        pltpu.VMEM((total, 128), BF),
        pltpu.SemaphoreType.DMA((sems,)),
        pltpu.SemaphoreType.DMA((sems,)),
    ]


def local(counts, features, labels, w_input, w_dilate4, w_dilate8, w_classes):
    chans, rows, cols = features.shape
    mid = w_input.shape[0]
    classes = w_classes.shape[0]
    wide = cols + 16
    flat = features.reshape(chans, rows * cols)
    vmem = pl.BlockSpec(memory_space=pltpu.VMEM)
    scratch = [
        pltpu.VMEM((rows + 24, cols + 32, mid), BF),
        pltpu.VMEM((rows + 24, wide, 3 * mid), BF),
        pltpu.VMEM((rows, cols, mid), F32),
        pltpu.VMEM((rows + 16, wide, mid), F32),
        pltpu.VMEM((rows + 16, wide, mid), BF),
        pltpu.VMEM((rows + 16, cols, 3 * mid), BF),
        pltpu.VMEM((8, 128), F32),
        pltpu.VMEM((rows + 24, cols + 32, mid), BF),
        pltpu.VMEM((rows + 24, wide, 3 * mid), BF),
        pltpu.VMEM((rows + 8, wide, mid), BF),
        pltpu.VMEM((rows, wide, mid), BF),
        pltpu.VMEM((rows + 8, cols, 3 * mid), BF),
        pltpu.VMEM((rows * cols, mid), BF),
        pltpu.VMEM((9 * mid, mid), BF),
        pltpu.VMEM((9 * mid, mid), BF),
    ]
    scratch += [pltpu.SemaphoreType.DMA((8,))] * 4
    scratch += reduce_scratch(9 * mid + classes, counts)
    scratch += reduce_scratch(9 * mid + chans, counts)
    return pl.pallas_call(
        functools.partial(kernel, counts, rows, cols),
        out_shape=(
            jax.ShapeDtypeStruct((mid, chans), F32),
            jax.ShapeDtypeStruct((mid, 9 * mid), F32),
            jax.ShapeDtypeStruct((mid, 9 * mid), F32),
            jax.ShapeDtypeStruct((classes, mid), F32),
        ),
        in_specs=[vmem] * 6,
        out_specs=(vmem,) * 4,
        scratch_shapes=scratch,
        compiler_params=pltpu.CompilerParams(
            collective_id=0, has_side_effects=True, vmem_limit_bytes=56 * 1024 * 1024
        ),
        cost_estimate=pl.CostEstimate(
            flops=6_000_000_000, bytes_accessed=8_000_000, transcendentals=1_000_000
        ),
    )(flat, labels, w_input, w_dilate4, w_dilate8, w_classes)


def solution(mesh):
    counts = (mesh.shape["rows"], mesh.shape["cols"])
    return jax.shard_map(
        functools.partial(local, counts),
        mesh=mesh,
        in_specs=(P(None, "rows", "cols"), P("rows", "cols"), P(), P(), P(), P()),
        out_specs=(P(), P(), P(), P()),
        check_vma=False,
    )
```

time: 340 us -> 106 us (0.31); the launches traced: 334 us -> 106 us
  waiting for transfers between devices: 110 us -> 0 us
  Pallas kernels: 0 us -> 94.2 us
  local copies, waits for them, and re-layouts: 88.1 us -> 11.1 us
  blocking collectives: 41.8 us -> 0 us
  matrix products: 31.1 us -> 0 us
  other arithmetic: 24.2 us -> 0 us
  starting transfers between devices: 24 us -> 0 us
  between operations: 14.8 us -> 0.65 us
    pallas_call x0 -> x1, Pallas kernels: none -> 94.2 us  [local(): pl.pallas_call(functools.partial(kernel, counts, rows, cols), out_shape=(...]
    psum x1 -> x0, waiting for transfers between devices: 93 us -> none  [local(): lax.psum((grad_input, grad_dilate4, grad_dilate8, grad_classes), ('rows',...]
    psum x1 -> x0, blocking collectives: 41.8 us -> none  [local(): lax.psum((grad_input, grad_dilate4, grad_dilate8, grad_classes), ('rows',...]
    unnamed x89 -> x7, local copies, waits for them, and re-layouts: 42.3 us -> 11.1 us
    dot_general x10 -> x0, matrix products: 31.1 us -> none  [the longest x4 16.2 us: pixel_contract(): lax.dot_general(left, right, (((1,), (1,)), ((), ())), preferred_element_...]
    concatenate x7 -> x0, local copies, waits for them, and re-layouts: 30.8 us -> none  [the longest x6 30.8 us: gather_taps(): stacked = jnp.concatenate(pieces, 0)]
    ppermute x8 -> x0, starting transfers between devices: 24 us -> none  [the longest x4 17 us: extended(): before = lax.ppermute(last, axis, up)]
    ppermute x8 -> x0, waiting for transfers between devices: 16.6 us -> none  [the longest x4 14.7 us: extended(): before = lax.ppermute(last, axis, up)]
  transfers between devices with their start and end apart: 9 -> 0, of which waited for: 4 -> 0; matrix products, arithmetic and copies ran while one was open for 8% -> 0% of each run, Pallas kernels for 0% -> 0%
where the time goes in v1:
time: 106 us
  Pallas kernels  94.2 us (89%)
  local copies, waits for them, and re-layouts  11.1 us (10%)
    pallas_call x1, Pallas kernels, local(): pl.pallas_call(functools.partial(kernel, counts, rows, cols), out_shape=(...  94.2 us
    unnamed x7, local copies, waits for them, and re-layouts  11.1 us

profile of v1, /device:TPU:1, one launch (start us, length us, event | category | flops | bytes accessed | tf_op | source)
XLA Modules:
  0.0 105.9 jit_solution(3605795390329232700)
XLA Ops:
  0.6 4.9 %copy.12 = bf16[96,8,16,128]{3,1,2,0:T(8,128)(2,1)} copy(bf16[96,8,16,128]{3,2,1,0:T(8,128)(2,1)} %bitcast.4) | data formatting | bytes 6291456
  5.5 94.2 %shard_map.93 = (f32[128,768]{1,0:T(8,128)}, f32[128,1152]{1,0:T(8,128)}, f32[128,1152]{1,0:T(8,128)}, f32[16,128]{1,0:T(8,128)}) custom-call(bf16[768,2048]{1,0:T(8,128)(2,1)} %bitcast.5, s32[16,128]{1,0:T(8,128)} %refs_1_.1, bf16[128,768]{1,0:T(8,128)(2,1)} %refs_2_.1, bf16[128,1152]{1,0:T(8,128)(2,1)} %refs_3_.1, bf16[128,1152]{1,0:T(8,128)(2,1)} %refs_4_.1, ...), custom_call_target="tpu_custom_call" | custom-call | flops 6000000000 | bytes 8000000 | tf_op jit(solution)/shard_map/pallas_call | solution.py:390
  99.7 0.0 copy-start
  99.7 1.8 %copy.17 = f32[128,768]{1,0:T(8,128)} copy(f32[128,768]{1,0:T(8,128)} %get-tuple-element.8) | data formatting | bytes 786432
  101.4 1.9 %copy.18 = f32[128,1152]{1,0:T(8,128)} copy(f32[128,1152]{1,0:T(8,128)} %get-tuple-element.9) | data formatting | bytes 1179648
  103.4 1.9 %copy.19 = f32[128,1152]{1,0:T(8,128)} copy(f32[128,1152]{1,0:T(8,128)} %get-tuple-element.10) | data formatting | bytes 1179648
  105.3 0.0 copy-done
  105.3 0.6 copy.20
Async XLA Ops:
  99.7 5.6 %copy-start = (f32[16,128]{1,0:T(8,128)S(1)}, f32[16,128]{1,0:T(8,128)}, u32[]{:S(2)}) copy-start(f32[16,128]{1,0:T(8,128)} %get-tuple-element.11) | copy-start | bytes 24580
